TPU v7x, 128 devices: a whole 4x4x4 slice. The times are simulated.
128 devices in a mesh: ctx: 16 (over y_lo, z, core), tp: 8 (over y_hi, x).
Axes of the slice: x: 4, y: 4 (y_hi: 2, y_lo: 2; y = y_hi * 2 + y_lo), z: 4, core: 2. Of those that a mesh axis runs over, the one named last changes fastest.
Arguments:
- tokens: bfloat16 [4096, 16384], P('tp', 'ctx'), may hold values from -6 to 6
- in_weight: bfloat16 [3, 4096, 4096], P(None, 'ctx', 'tp'), may hold values from -0.09375 to 0.09375
- short_taps: float32 [3, 4096, 3], P(None, 'tp'), may hold values from -3 to 3
- long_filter: float32 [4096, 16384], P('tp', 'ctx'), may hold values from -2 to 2
- skip_gain: float32 [4096], P('tp'), may hold values from -4 to 4
- out_weight: bfloat16 [4096, 4096], P('tp', 'ctx'), may hold values from -0.125 to 0.125
Outputs:
- layer_out: bfloat16 [4096, 16384], P('tp', 'ctx')
All inputs are finite; a program needn't handle non-finite values.
Results may differ from a plain program's by a relative error of at most 0.02.
Values may be sent and summed in bfloat16 or wider, within the bound.
A program may use at most 128 MiB of HBM per device.

v0:
```python
import math
import jax
import jax.numpy as jnp
from jax import lax
from jax.sharding import PartitionSpec as P

HIGHEST = lax.Precision.HIGHEST


def passed_along(shard, axis, by):
    count = lax.axis_size(axis)
    pairs = [(i, i + by) for i in range(count) if 0 <= i + by < count]
    return lax.ppermute(shard, axis, pairs)


def factor_length(full_len):
    inner_len = 1
    while inner_len * inner_len * 4 <= full_len and full_len % (inner_len * 2) == 0:
        inner_len = inner_len * 2
    return (inner_len, full_len // inner_len)


def phase_table(rows_count, cols_count, period):
    row_ids = jnp.arange(rows_count, dtype=jnp.int32)[:, None]
    col_ids = jnp.arange(cols_count, dtype=jnp.int32)[None, :]
    angles = (row_ids * col_ids % period).astype(jnp.float32) * (2.0 * math.pi / period)
    return (jnp.cos(angles), jnp.sin(angles))


def make_tables(full_len):
    inner_len, outer_len = factor_length(full_len)
    cos_inner, sin_inner = phase_table(inner_len, inner_len, inner_len)
    cos_outer, sin_outer = phase_table(outer_len // 2, outer_len, outer_len)
    cos_twist, sin_twist = phase_table(outer_len, inner_len, full_len)
    return (cos_inner, sin_inner, cos_outer, sin_outer, cos_twist, sin_twist)


def spectrum(signal, tables):
    cos_inner, sin_inner, cos_outer, sin_outer, cos_twist, sin_twist = tables
    channels = signal.shape[0]
    grid_view = signal.reshape(channels, cos_outer.shape[0], cos_inner.shape[0])
    part_re = jnp.einsum("cmn,mk->ckn", grid_view, cos_outer, precision=HIGHEST)
    part_im = -jnp.einsum("cmn,mk->ckn", grid_view, sin_outer, precision=HIGHEST)
    twist_re = part_re * cos_twist + part_im * sin_twist
    twist_im = part_im * cos_twist - part_re * sin_twist
    freq_re = jnp.einsum("ckn,nj->ckj", twist_re, cos_inner, precision=HIGHEST) + jnp.einsum(
        "ckn,nj->ckj", twist_im, sin_inner, precision=HIGHEST
    )
    freq_im = jnp.einsum("ckn,nj->ckj", twist_im, cos_inner, precision=HIGHEST) - jnp.einsum(
        "ckn,nj->ckj", twist_re, sin_inner, precision=HIGHEST
    )
    return (freq_re, freq_im)


def spectrum_back(freq_re, freq_im, tables):
    cos_inner, sin_inner, cos_outer, sin_outer, cos_twist, sin_twist = tables
    mix_re = jnp.einsum("ckj,jn->ckn", freq_re, cos_inner, precision=HIGHEST) - jnp.einsum(
        "ckj,jn->ckn", freq_im, sin_inner, precision=HIGHEST
    )
    mix_im = jnp.einsum("ckj,jn->ckn", freq_im, cos_inner, precision=HIGHEST) + jnp.einsum(
        "ckj,jn->ckn", freq_re, sin_inner, precision=HIGHEST
    )
    turn_re = mix_re * cos_twist - mix_im * sin_twist
    turn_im = mix_im * cos_twist + mix_re * sin_twist
    channels = freq_re.shape[0]
    length = cos_outer.shape[0] * cos_inner.shape[0]
    norm_factor = 1.0 / (cos_outer.shape[1] * cos_inner.shape[0])
    real_out = jnp.einsum("ckn,mk->cmn", turn_re, cos_outer, precision=HIGHEST) - jnp.einsum(
        "ckn,mk->cmn", turn_im, sin_outer, precision=HIGHEST
    )
    real_out = real_out.reshape(channels, length) * norm_factor
    return real_out


def per_device(tokens, in_weight, short_taps, long_filter, skip_gain, out_weight):
    steps_dev = tokens.shape[1]
    filter_groups = lax.all_to_all(
        long_filter.astype(jnp.bfloat16), "ctx", split_axis=0, concat_axis=1, tiled=True
    ).astype(long_filter.dtype)
    features_all = lax.all_gather(tokens, "tp", axis=0, tiled=True)
    sources = (features_all,)
    shard_rows = lax.all_gather(in_weight, "ctx", axis=1, tiled=True)
    results = tuple(
        (
            jnp.einsum("sic,it->sct", shard_rows, source, preferred_element_type=jnp.float32)
            for source in sources
        )
    )
    projected = results[0]
    before = passed_along(projected[:, :, steps_dev - 2 :], "ctx", 1)
    prev_one = jnp.concatenate([before[:, :, 1:], projected[:, :, :-1]], axis=2)
    prev_two = jnp.concatenate([before, projected[:, :, :-2]], axis=2)
    mixed_short = (
        short_taps[:, :, 0:1] * projected
        + short_taps[:, :, 1:2] * prev_one
        + short_taps[:, :, 2:3] * prev_two
    )
    gated_rows = (mixed_short[1] * mixed_short[2]).astype(jnp.bfloat16)
    signal = lax.all_to_all(gated_rows, "ctx", split_axis=0, concat_axis=1, tiled=True)
    tables = make_tables(2 * signal.shape[1])
    sig_re, sig_im = spectrum(signal.astype(jnp.float32), tables)
    fil_re, fil_im = spectrum(filter_groups, tables)
    prod_re = sig_re * fil_re - sig_im * fil_im
    prod_im = sig_re * fil_im + sig_im * fil_re
    long_rows = spectrum_back(prod_re, prod_im, tables)
    long_rows = long_rows.astype(jnp.bfloat16)
    returned = lax.all_to_all(long_rows, "ctx", split_axis=1, concat_axis=0, tiled=True)
    hidden = (
        (returned.astype(jnp.float32) + skip_gain[:, None] * gated_rows.astype(jnp.float32))
        * mixed_short[0]
    ).astype(jnp.bfloat16)
    whole_out = lax.all_gather(out_weight, "ctx", axis=1, tiled=True)
    return lax.psum_scatter(
        jnp.einsum("cd,ct->dt", whole_out, hidden, preferred_element_type=jnp.float32).astype(
            jnp.bfloat16
        ),
        "tp",
        scatter_dimension=0,
        tiled=True,
    )


def solution(mesh):
    placed = (
        P("tp", "ctx"),
        P(None, "ctx", "tp"),
        P(None, "tp", None),
        P("tp", "ctx"),
        P("tp"),
        P("tp", "ctx"),
    )
    return jax.shard_map(
        per_device, mesh=mesh, in_specs=placed, out_specs=P("tp", "ctx"), check_vma=False
    )
```

profile of v0, /device:TPU:1, one launch (start us, length us, event | category | flops | bytes accessed | tf_op | source)
XLA Modules:
  0.0 480.2 jit_solution(12676117775673328608)
XLA Ops:
  10.8 7.8 %all-to-all-start.1 = ((bf16[16,32,1024]{2,1,0:T(8,128)(2,1)}), bf16[16,32,1024]{2,1,0:T(8,128)(2,1)S(1)}, u32[]{:S(2)}, u32[]{:S(2)}) async-start(bf16[16,32,1024]{2,1,0:T(8,128)(2,1)} %bitcast.11), calls=%async_computation.1 | async-start | bytes 2097152 | tf_op jit(solution)/shard_map/all_to_all | solution.py:77
  20.0 19.7 %all-to-all-done.1 = bf16[16,32,1024]{2,1,0:T(8,128)(2,1)S(1)} async-done(((bf16[16,32,1024]{2,1,0:T(8,128)(2,1)}), bf16[16,32,1024]{2,1,0:T(8,128)(2,1)S(1)}, u32[]{:S(2)}, u32[]{:S(2)}) %all-to-all-start.1) | async-done | bytes 1048608 | tf_op jit(solution)/shard_map/all_to_all | solution.py:77
  47.4 5.6 %fusion.6 = f32[32,256,128]{2,1,0:T(8,128)} fusion(f32[256,32,128]{2,0,1:T(8,128)S(1)} %fusion.64, f32[256,32,128]{2,0,1:T(8,128)S(1)} %fusion.60, f32[256,128]{1,0:T(8,128)S(1)} %get-tuple-element.12, f32[256,128]{1,0:T(8,128)S(1)} %get-tuple-element.13), kind=kOutput, calls=%fused_computation.9 | convolution fusion | flops 1615036416 | bytes 12845056 | tf_op jit(solution)/shard_map/ckn,nj->ckj/dot_general | solution.py:46
  53.0 74.5 %all-gather.6.cloned.1.call-done = bf16[4096,1024]{1,0:T(8,128)(2,1)} async-done(((bf16[512,1024]{1,0:T(8,128)(2,1)}), bf16[4096,1024]{1,0:T(8,128)(2,1)}) %all-gather.6.cloned.1.call-update) | async-done | bytes 8388624 | tf_op jit(solution)/shard_map/all_gather | solution.py:80
  127.5 79.9 %all-gather.4.cloned.1.call-done = bf16[3,4096,512]{1,2,0:T(8,128)(2,1)} async-done(((bf16[3,256,512]{1,2,0:T(8,128)(2,1)}), bf16[3,4096,512]{1,2,0:T(8,128)(2,1)}) %all-gather.4.cloned.1.call-update) | async-done | bytes 12582928 | tf_op jit(solution)/shard_map/all_gather | solution.py:82
  207.3 16.7 %fusion = f32[3,512,1024]{2,1,0:T(8,128)S(1)} fusion(bf16[3,4096,512]{1,2,0:T(8,128)(2,1)} %all-gather.4.cloned.1.call-done, bf16[4096,1024]{1,0:T(8,128)(2,1)} %all-gather.6.cloned.1.call-done), kind=kOutput, calls=%fused_computation | convolution fusion | flops 12884901888 | bytes 27262976 | tf_op jit(solution)/shard_map/sic,it->sct/dot_general | solution.py:85
  230.0 8.5 %fusion.34 = f32[32,256,128]{2,1,0:T(8,128)} fusion(f32[32,256,128]{2,1,0:T(8,128)} %fusion.6, f32[256,32,128]{2,0,1:T(8,128)} %copy-done, f32[256,32,128]{2,0,1:T(8,128)} %copy-done.2, f32[256,128]{1,0:T(8,128)S(1)} %get-tuple-element.12, f32[256,128]{1,0:T(8,128)S(1)} %get-tuple-element.13), kind=kOutput, calls=%fused_computation.39 | convolution fusion | flops 1616084992 | bytes 17039360 | tf_op jit(solution)/shard_map/ckn,nj->ckj/dot_general | solution.py:46
  239.1 9.3 %fusion.3 = f32[3,512,1024]{2,1,0:T(8,128)S(1)} fusion(f32[3,512,1023]{2,1,0:T(8,128)} %bitcast.120, f32[3,512,1]{2,1,0:T(8,128)S(1)} %copy.27, f32[3,512,1022]{2,1,0:T(8,128)} %bitcast.121, f32[3,512,2]{2,1,0:T(8,128)S(1)} %copy.28, f32[3,512,1024]{2,1,0:T(8,128)} %copy-done.4, f32[3,512]{1,0:T(4,128)S(1)} %get-tuple-element.10, ...), kind=kLoop, calls=%fused_computation.5 | loop fusion | flops 11010048 | bytes 25184256 | tf_op jit(solution)/shard_map/add | solution.py:94
  252.3 4.5 all-to-all-start
  256.9 6.8 %fusion.4 = f32[32,256,128]{2,1,0:T(8,128)S(1)} fusion(f32[256,32,128]{2,0,1:T(8,128)} %copy-done, f32[256,32,128]{2,0,1:T(8,128)} %copy-done.2, f32[256,128]{1,0:T(8,128)S(1)} %get-tuple-element.12, f32[256,128]{1,0:T(8,128)S(1)} %get-tuple-element.13), kind=kOutput, calls=%fused_computation.7 | convolution fusion | flops 1615036416 | bytes 12845056 | tf_op jit(solution)/shard_map/ckn,nj->ckj/dot_general | solution.py:49
  263.7 5.7 %fusion.37 = f32[32,256,128]{2,1,0:T(8,128)} fusion(f32[32,256,128]{2,1,0:T(8,128)S(1)} %fusion.4, f32[256,32,128]{2,0,1:T(8,128)S(1)} %copy-done.1, f32[256,32,128]{2,0,1:T(8,128)S(1)} %copy-done.3, f32[256,128]{1,0:T(8,128)S(1)} %get-tuple-element.12, f32[256,128]{1,0:T(8,128)S(1)} %get-tuple-element.13), kind=kOutput, calls=%fused_computation.40 | convolution fusion | flops 1616084992 | bytes 17039360 | tf_op jit(solution)/shard_map/ckn,nj->ckj/dot_general | solution.py:49
  278.8 4.3 fusion.14
  283.2 5.5 %fusion.12 = f32[32,256,128]{2,1,0:T(8,128)S(1)} fusion(f32[256,32,128]{2,0,1:T(8,128)S(1)} %fusion.66, f32[256,32,128]{2,0,1:T(8,128)S(1)} %fusion.62, f32[256,128]{1,0:T(8,128)} %copy-done.6, f32[256,128]{1,0:T(8,128)} %copy-done.9), kind=kOutput, calls=%fused_computation.15 | convolution fusion | flops 1615036416 | bytes 12845056 | tf_op jit(solution)/shard_map/ckn,nj->ckj/dot_general | solution.py:49
  288.7 5.7 %fusion.28 = f32[32,256,128]{2,1,0:T(8,128)} fusion(f32[32,256,128]{2,1,0:T(8,128)S(1)} %fusion.14, f32[256,32,128]{2,0,1:T(8,128)S(1)} %fusion.66, f32[256,32,128]{2,0,1:T(8,128)S(1)} %fusion.62, f32[256,128]{1,0:T(8,128)S(1)} %copy-done.7, f32[256,128]{1,0:T(8,128)S(1)} %copy-done.10), kind=kOutput, calls=%fused_computation.37 | convolution fusion | flops 1616084992 | bytes 17039360 | tf_op jit(solution)/shard_map/ckn,nj->ckj/dot_general | solution.py:46
  294.4 8.4 %multiply_add_fusion = (f32[32,256,128]{2,1,0:T(8,128)S(1)}, f32[32,256,128]{2,1,0:T(8,128)S(1)}) fusion(f32[32,256,128]{2,1,0:T(8,128)} %fusion.34, f32[32,256,128]{2,1,0:T(8,128)} %fusion.28, f32[32,256,128]{2,1,0:T(8,128)} %fusion.37, f32[32,256,128]{2,1,0:T(8,128)S(1)} %fusion.12, f32[256,128]{1,0:T(8,128)} %copy-done.6, ...), kind=kOutput, calls=%fused_computation.31 | convolution fusion | flops 1622376448 | bytes 33816576 | tf_op jit(solution)/shard_map/ckn,nj->ckj/dot_general | solution.py:49
  302.8 3.7 fusion.86
  306.5 3.7 fusion.84
  310.1 3.7 convolution_subtract_fusion
  313.8 3.9 convolution_add_fusion
  321.0 3.4 fusion.50
  325.5 19.1 %all_to_all.39 = bf16[32,16,1024]{2,0,1:T(8,128)(2,1)S(1)} all-to-all(bf16[32,16,1024]{2,0,1:T(8,128)(2,1)S(1)} %copy.35), channel_id=1, replica_groups=mesh['ctx'=16,'tp'=8] {'ctx'}, dimensions={1} | all-to-all | bytes 2097152 | tf_op jit(solution)/shard_map/all_to_all | solution.py:107
  344.6 3.4 fusion.41
  348.0 9.0 %convert_bitcast_fusion = bf16[4096,1024]{0,1:T(8,128)(2,1)} fusion(bf16[512,1024]{1,0:T(8,128)(2,1)S(1)} %fusion.41, bf16[512,4096]{1,0:T(8,128)(2,1)} %all-gather.8.cloned.1.call-done), kind=kOutput, calls=%fused_computation.2 | convolution fusion | flops 4299161600 | bytes 13631488 | tf_op jit(solution)/shard_map/cd,ct->dt/dot_general | solution.py:114
  357.0 113.9 %reduce-scatter.2.cloned.1.call-done = bf16[512,1024]{0,1:T(8,128)(2,1)} async-done(((bf16[4096,1024]{0,1:T(8,128)(2,1)}), bf16[512,1024]{0,1:T(8,128)(2,1)}) %reduce-scatter.2.cloned.1.call-update) | async-done | bytes 1048592 | tf_op jit(solution)/shard_map/reduce_scatter | solution.py:113
  (66 shorter events, 39.8 us)
Async XLA Ops:
  6.5 3.1 copy-start.12
  6.5 120.9 %all-gather.6.cloned.1.call-start = ((), (), s32[]{:S(2)}) async-start(), calls=%async_computation.5 | async-start | bytes 9437184 | tf_op jit(solution)/shard_map/all_gather | solution.py:80
  7.3 12.1 %copy-start.13 = (f32[3,512,3]{1,2,0:T(4,128)S(1)}, f32[3,512,3]{1,2,0:T(4,128)}, u32[]{:S(2)}) copy-start(f32[3,512,3]{1,2,0:T(4,128)} %param.8) | copy-start | bytes 55300
  7.3 200.1 %all-gather.4.cloned.1.call-start = ((), (), s32[]{:S(2)}) async-start(), calls=%async_computation.4 | async-start | bytes 13369344 | tf_op jit(solution)/shard_map/all_gather | solution.py:82
  10.8 28.8 %all-to-all-start.1 = ((bf16[16,32,1024]{2,1,0:T(8,128)(2,1)}), bf16[16,32,1024]{2,1,0:T(8,128)(2,1)S(1)}, u32[]{:S(2)}, u32[]{:S(2)}) async-start(bf16[16,32,1024]{2,1,0:T(8,128)(2,1)} %bitcast.11), calls=%async_computation.1 | async-start | bytes 2097152 | tf_op jit(solution)/shard_map/all_to_all | solution.py:77
  18.6 329.4 %all-gather.8.cloned.1.call-start = ((), (), s32[]{:S(2)}) async-start(), calls=%async_computation.6 | async-start | bytes 4456448 | tf_op jit(solution)/shard_map/all_gather | solution.py:112
  20.0 258.9 %copy-start.6 = (f32[256,128]{1,0:T(8,128)}, f32[256,128]{1,0:T(8,128)S(1)}, u32[]{:S(2)}) copy-start(f32[256,128]{1,0:T(8,128)S(1)} %get-tuple-element.12) | copy-start | bytes 393220
  20.0 258.9 %copy-start.9 = (f32[256,128]{1,0:T(8,128)}, f32[256,128]{1,0:T(8,128)S(1)}, u32[]{:S(2)}) copy-start(f32[256,128]{1,0:T(8,128)S(1)} %get-tuple-element.13) | copy-start | bytes 393220
  43.1 2.4 copy-start
  45.4 2.0 copy-start.2
  224.1 2.6 copy-start.4
  227.2 11.3 %collective-permute-start = (f32[3,512,2]{1,2,0:T(2,128)S(1)}, f32[3,512,2]{1,2,0:T(2,128)S(1)}, u32[]{:S(2)}, u32[]{:S(2)}) collective-permute-start(f32[3,512,2]{1,2,0:T(2,128)S(1)} %copy.26), channel_id=1, source_target_pairs={{0,8},{8,16},{16,24},{24,32},{32,40},{40,48},{48,56},{56,64},{64,7... | collective-permute-start | bytes 36872 | tf_op jit(solution)/shard_map/ppermute | solution.py:13
  248.4 2.6 copy-start.5
  252.3 20.3 %all-to-all-start = ((bf16[16,32,1024]{2,1,0:T(8,128)(2,1)}), bf16[16,32,1024]{2,1,0:T(8,128)(2,1)S(1)}, u32[]{:S(2)}, u32[]{:S(2)}) async-start(bf16[16,32,1024]{2,1,0:T(8,128)(2,1)} %bitcast.3), calls=%async_computation | async-start | bytes 2097152 | tf_op jit(solution)/shard_map/all_to_all | solution.py:99
  256.9 214.1 %reduce-scatter.2.cloned.1.call-start = ((), (), s32[]{:S(2)}) async-start(), calls=%async_computation.7 | async-start | bytes 9437184 | tf_op jit(solution)/shard_map/reduce_scatter | solution.py:113
  256.9 6.8 %copy-start.1 = (f32[256,32,128]{2,0,1:T(8,128)S(1)}, f32[256,32,128]{2,0,1:T(8,128)}, u32[]{:S(2)}) copy-start(f32[256,32,128]{2,0,1:T(8,128)} %copy-done) | copy-start | bytes 12582916
  256.9 6.8 %copy-start.3 = (f32[256,32,128]{2,0,1:T(8,128)S(1)}, f32[256,32,128]{2,0,1:T(8,128)}, u32[]{:S(2)}) copy-start(f32[256,32,128]{2,0,1:T(8,128)} %copy-done.2) | copy-start | bytes 12582916
  283.2 5.5 %copy-start.7 = (f32[256,128]{1,0:T(8,128)S(1)}, f32[256,128]{1,0:T(8,128)}, u32[]{:S(2)}) copy-start(f32[256,128]{1,0:T(8,128)} %copy-done.6) | copy-start | bytes 393220
  283.2 5.5 %copy-start.10 = (f32[256,128]{1,0:T(8,128)S(1)}, f32[256,128]{1,0:T(8,128)}, u32[]{:S(2)}) copy-start(f32[256,128]{1,0:T(8,128)} %copy-done.9) | copy-start | bytes 393220
  313.8 3.9 copy-start.8
  313.8 3.9 copy-start.11
  324.4 20.2 %copy-start.14 = (f32[512]{0:T(512)S(1)}, f32[512]{0:T(512)}, u32[]{:S(2)}) copy-start(f32[512]{0:T(512)} %param.10) | copy-start | bytes 6148
Sparse Core Ops, SparseCore 0:
  9.7 117.7 all-gather.5
  129.1 78.2 all-gather.3
  209.0 45.4 all-gather.7
  357.2 113.7 reduce-scatter.1
where the time goes:
time: 489 us; the launch traced here: 480 us
  waiting for transfers between devices  293 us (60%)
  matrix products  107 us (22%)
  blocking collectives  19.1 us (4%)
  local copies, waits for them, and re-layouts  16.7 us (3%)
  other arithmetic  15.6 us (3%)
  starting transfers between devices  15.3 us (3%)
  between operations  14 us (3%)
    reduce_scatter x1, waiting for transfers between devices, per_device(): lax.psum_scatter(jnp.einsum('cd,ct->dt', whole_out, hidden, preferred_ele...  114 us
    all_gather x1, waiting for transfers between devices, per_device(): shard_rows = lax.all_gather(in_weight, 'ctx', axis=1, tiled=True)  79.9 us
    all_gather x1, waiting for transfers between devices, per_device(): features_all = lax.all_gather(tokens, 'tp', axis=0, tiled=True)  74.5 us
    all_to_all x1, waiting for transfers between devices, per_device(): lax.all_to_all(long_filter.astype(jnp.bfloat16), 'ctx', split_axis=0, con...  19.7 us
    all_to_all x1, blocking collectives, per_device(): lax.all_to_all(long_rows, 'ctx', split_axis=1, concat_axis=0, tiled=True)  19.1 us
    dot_general x1, matrix products, per_device(): jnp.einsum('sic,it->sct', shard_rows, source, preferred_element_type=jnp....  16.7 us
    dot_general x2, matrix products, spectrum(): jnp.einsum('ckn,nj->ckj', twist_re, sin_inner, precision=HIGHEST)  14.1 us
    dot_general x2, matrix products, spectrum(): jnp.einsum('ckn,nj->ckj', twist_re, cos_inner, precision=HIGHEST)  14.1 us
  transfers between devices with their start and end apart: 7, of which 5 were waited for; matrix products, arithmetic and copies ran while one was open for 25% of the time, Pallas kernels for 0%

commit v1 on v0

--- a/solution.py
+++ b/solution.py
@@ -79,7 +79,9 @@
     ).astype(long_filter.dtype)
     features_all = lax.all_gather(tokens, "tp", axis=0, tiled=True)
     sources = (features_all,)
-    shard_rows = lax.all_gather(in_weight, "ctx", axis=1, tiled=True)
+    shard_rows = jnp.concatenate(
+        lax.all_to_all(jnp.stack([in_weight] * lax.axis_size("ctx")), "ctx", 0, 0), axis=1
+    )
     results = tuple(
         (
             jnp.einsum("sic,it->sct", shard_rows, source, preferred_element_type=jnp.float32)

time: 489 us -> 561 us (1.15)
  waiting for transfers between devices: 293 us -> 338 us
  local copies, waits for them, and re-layouts: 16.7 us -> 31.3 us
  starting transfers between devices: 15.3 us -> 25.2 us
    all_to_all x0 -> x1, waiting for transfers between devices: none -> 199 us  [per_device(): lax.all_to_all(jnp.stack([in_weight] * lax.axis_size('ctx')), 'ctx', 0, 0)]
    all_gather x1 -> x0, waiting for transfers between devices: 79.9 us -> none  [per_device(): shard_rows = lax.all_gather(in_weight, 'ctx', axis=1, tiled=True)]
    all_gather x1, waiting for transfers between devices: 74.5 us -> 0.01 us  [per_device(): features_all = lax.all_gather(tokens, 'tp', axis=0, tiled=True)]
    reshape x0 -> x1, local copies, waits for them, and re-layouts: none -> 10.8 us  [per_device(): jnp.concatenate(lax.all_to_all(jnp.stack([in_weight] * lax.axis_size('ctx...]
    all_to_all x0 -> x1, starting transfers between devices: none -> 6.53 us  [per_device(): lax.all_to_all(jnp.stack([in_weight] * lax.axis_size('ctx')), 'ctx', 0, 0)]
    another operation x0 -> x1, local copies, waits for them, and re-layouts: none -> 6 us  [per_device(): jnp.stack([in_weight] * lax.axis_size('ctx'))]
  transfers between devices with their start and end apart: 7 -> 7, of which waited for: 5 -> 4; matrix products, arithmetic and copies ran while one was open for 25% -> 25% of each run, Pallas kernels for 0% -> 0%
where the time goes in v1:
time: 561 us; the launch traced here: 551 us
  waiting for transfers between devices  338 us (60%)
  matrix products  107 us (19%)
  local copies, waits for them, and re-layouts  31.3 us (6%)
  starting transfers between devices  25.2 us (4%)
  blocking collectives  19.1 us (3%)
  other arithmetic  16.9 us (3%)
  between operations  14 us (2%)
    all_to_all x1, waiting for transfers between devices, per_device(): lax.all_to_all(jnp.stack([in_weight] * lax.axis_size('ctx')), 'ctx', 0, 0)  199 us
    reduce_scatter x1, waiting for transfers between devices, per_device(): lax.psum_scatter(jnp.einsum('cd,ct->dt', whole_out, hidden, preferred_ele...  114 us
    all_to_all x1, waiting for transfers between devices, per_device(): lax.all_to_all(long_filter.astype(jnp.bfloat16), 'ctx', split_axis=0, con...  19.9 us
    all_to_all x1, blocking collectives, per_device(): lax.all_to_all(long_rows, 'ctx', split_axis=1, concat_axis=0, tiled=True)  19.1 us
    dot_general x1, matrix products, per_device(): jnp.einsum('sic,it->sct', shard_rows, source, preferred_element_type=jnp....  16.7 us
    dot_general x2, matrix products, spectrum(): jnp.einsum('ckn,nj->ckj', twist_re, sin_inner, precision=HIGHEST)  14.2 us
    dot_general x2, matrix products, spectrum(): jnp.einsum('ckn,nj->ckj', twist_re, cos_inner, precision=HIGHEST)  14.2 us
    dot_general x2, matrix products, spectrum(): jnp.einsum('ckn,nj->ckj', twist_im, cos_inner, precision=HIGHEST)  12.2 us
  transfers between devices with their start and end apart: 7, of which 4 were waited for; matrix products, arithmetic and copies ran while one was open for 25% of the time, Pallas kernels for 0%

profile of v1, /device:TPU:1, one launch (start us, length us, event | category | flops | bytes accessed | tf_op | source)
XLA Modules:
  0.0 551.3 jit_solution(4148582532454923882)
XLA Ops:
  10.0 7.8 %all-to-all-start.2 = ((bf16[16,32,1024]{2,1,0:T(8,128)(2,1)}), bf16[16,32,1024]{2,1,0:T(8,128)(2,1)S(1)}, u32[]{:S(2)}, u32[]{:S(2)}) async-start(bf16[16,32,1024]{2,1,0:T(8,128)(2,1)} %bitcast.12), calls=%async_computation.2 | async-start | bytes 2097152 | tf_op jit(solution)/shard_map/all_to_all | solution.py:77
  18.1 19.9 %all-to-all-done.2 = bf16[16,32,1024]{2,1,0:T(8,128)(2,1)S(1)} async-done(((bf16[16,32,1024]{2,1,0:T(8,128)(2,1)}), bf16[16,32,1024]{2,1,0:T(8,128)(2,1)S(1)}, u32[]{:S(2)}, u32[]{:S(2)}) %all-to-all-start.2) | async-done | bytes 1048608 | tf_op jit(solution)/shard_map/all_to_all | solution.py:77
  38.0 6.0 %stack.2 = bf16[16,3,256,512]{2,3,1,0:T(8,128)(2,1)} broadcast(bf16[3,256,512]{1,2,0:T(8,128)(2,1)S(1)} %copy.25), dimensions={1,2,3} | broadcast | bytes 13369344 | tf_op jit(solution)/shard_map/stack | solution.py:83
  44.0 6.5 %all-to-all-start = ((bf16[16,3,256,512]{2,3,1,0:T(8,128)(2,1)}), bf16[16,3,256,512]{2,3,1,0:T(8,128)(2,1)}, u32[]{:S(2)}, u32[]{:S(2)}) async-start(bf16[16,3,256,512]{2,3,1,0:T(8,128)(2,1)} %stack.2), calls=%async_computation | async-start | bytes 25165824 | tf_op jit(solution)/shard_map/all_to_all | solution.py:83
  59.7 5.7 %fusion.6 = f32[32,256,128]{2,1,0:T(8,128)} fusion(f32[256,32,128]{2,0,1:T(8,128)S(1)} %fusion.64, f32[256,32,128]{2,0,1:T(8,128)S(1)} %fusion.60, f32[256,128]{1,0:T(8,128)S(1)} %get-tuple-element.12, f32[256,128]{1,0:T(8,128)S(1)} %get-tuple-element.13), kind=kOutput, calls=%fused_computation.9 | convolution fusion | flops 1615036416 | bytes 12845056 | tf_op jit(solution)/shard_map/ckn,nj->ckj/dot_general | solution.py:46
  65.3 198.9 %all-to-all-done = bf16[16,3,256,512]{2,3,1,0:T(8,128)(2,1)} async-done(((bf16[16,3,256,512]{2,3,1,0:T(8,128)(2,1)}), bf16[16,3,256,512]{2,3,1,0:T(8,128)(2,1)}, u32[]{:S(2)}, u32[]{:S(2)}) %all-to-all-start) | async-done | bytes 12582944 | tf_op jit(solution)/shard_map/all_to_all | solution.py:83
  264.2 10.8 %copy.49 = bf16[16,3,64,8,256]{4,3,0,2,1:T(8,128)(2,1)} copy(bf16[16,3,64,8,256]{4,3,2,1,0:T(8,128)(2,1)} %bitcast.29) | data formatting | bytes 25165824 | tf_op jit(solution)/shard_map/reshape | solution.py:82
  275.0 16.7 %fusion = f32[3,512,1024]{2,1,0:T(8,128)S(1)} fusion(bf16[3,4096,512]{1,2,0:T(8,128)(2,1)} %bitcast.125, bf16[4096,1024]{1,0:T(8,128)(2,1)} %all-gather.3.cloned.1.call-done), kind=kOutput, calls=%fused_computation | convolution fusion | flops 12884901888 | bytes 27262976 | tf_op jit(solution)/shard_map/sic,it->sct/dot_general | solution.py:87
  297.0 8.5 %fusion.34 = f32[32,256,128]{2,1,0:T(8,128)} fusion(f32[32,256,128]{2,1,0:T(8,128)} %fusion.6, f32[256,32,128]{2,0,1:T(8,128)} %copy-done, f32[256,32,128]{2,0,1:T(8,128)} %copy-done.2, f32[256,128]{1,0:T(8,128)S(1)} %get-tuple-element.12, f32[256,128]{1,0:T(8,128)S(1)} %get-tuple-element.13), kind=kOutput, calls=%fused_computation.39 | convolution fusion | flops 1616084992 | bytes 17039360 | tf_op jit(solution)/shard_map/ckn,nj->ckj/dot_general | solution.py:46
  306.1 8.9 %fusion.3 = f32[3,512,1024]{2,1,0:T(8,128)S(1)} fusion(f32[3,512,1023]{2,1,0:T(8,128)} %bitcast.123, f32[3,512,1]{2,1,0:T(8,128)S(1)} %copy.28, f32[3,512,1022]{2,1,0:T(8,128)} %bitcast.124, f32[3,512,2]{2,1,0:T(8,128)S(1)} %copy.29, f32[3,512,1024]{2,1,0:T(8,128)} %copy-done.4, f32[3,512]{1,0:T(4,128)S(1)} %get-tuple-element.10, ...), kind=kLoop, calls=%fused_computation.5 | loop fusion | flops 11010048 | bytes 25184256 | tf_op jit(solution)/shard_map/add | solution.py:96
  319.0 8.6 %all-to-all-start.1 = ((bf16[16,32,1024]{2,1,0:T(8,128)(2,1)}), bf16[16,32,1024]{2,1,0:T(8,128)(2,1)S(1)}, u32[]{:S(2)}, u32[]{:S(2)}) async-start(bf16[16,32,1024]{2,1,0:T(8,128)(2,1)} %bitcast.4), calls=%async_computation.1 | async-start | bytes 2097152 | tf_op jit(solution)/shard_map/all_to_all | solution.py:101
  327.7 6.8 %fusion.4 = f32[32,256,128]{2,1,0:T(8,128)S(1)} fusion(f32[256,32,128]{2,0,1:T(8,128)} %copy-done, f32[256,32,128]{2,0,1:T(8,128)} %copy-done.2, f32[256,128]{1,0:T(8,128)S(1)} %get-tuple-element.12, f32[256,128]{1,0:T(8,128)S(1)} %get-tuple-element.13), kind=kOutput, calls=%fused_computation.7 | convolution fusion | flops 1615036416 | bytes 12845056 | tf_op jit(solution)/shard_map/ckn,nj->ckj/dot_general | solution.py:49
  334.5 5.8 %fusion.37 = f32[32,256,128]{2,1,0:T(8,128)} fusion(f32[32,256,128]{2,1,0:T(8,128)S(1)} %fusion.4, f32[256,32,128]{2,0,1:T(8,128)S(1)} %copy-done.1, f32[256,32,128]{2,0,1:T(8,128)S(1)} %copy-done.3, f32[256,128]{1,0:T(8,128)S(1)} %get-tuple-element.12, f32[256,128]{1,0:T(8,128)S(1)} %get-tuple-element.13), kind=kOutput, calls=%fused_computation.40 | convolution fusion | flops 1616084992 | bytes 17039360 | tf_op jit(solution)/shard_map/ckn,nj->ckj/dot_general | solution.py:49
  349.6 4.3 fusion.14
  353.9 5.5 fusion.12
  359.4 5.7 %fusion.28 = f32[32,256,128]{2,1,0:T(8,128)} fusion(f32[32,256,128]{2,1,0:T(8,128)S(1)} %fusion.14, f32[256,32,128]{2,0,1:T(8,128)S(1)} %fusion.66, f32[256,32,128]{2,0,1:T(8,128)S(1)} %fusion.62, f32[256,128]{1,0:T(8,128)S(1)} %copy-done.7, f32[256,128]{1,0:T(8,128)S(1)} %copy-done.10), kind=kOutput, calls=%fused_computation.37 | convolution fusion | flops 1616084992 | bytes 17039360 | tf_op jit(solution)/shard_map/ckn,nj->ckj/dot_general | solution.py:46
  365.2 8.4 %multiply_add_fusion = (f32[32,256,128]{2,1,0:T(8,128)S(1)}, f32[32,256,128]{2,1,0:T(8,128)S(1)}) fusion(f32[32,256,128]{2,1,0:T(8,128)} %fusion.34, f32[32,256,128]{2,1,0:T(8,128)} %fusion.28, f32[32,256,128]{2,1,0:T(8,128)} %fusion.37, f32[32,256,128]{2,1,0:T(8,128)S(1)} %fusion.12, f32[256,128]{1,0:T(8,128)} %copy-done.6, ...), kind=kOutput, calls=%fused_computation.31 | convolution fusion | flops 1622376448 | bytes 33816576 | tf_op jit(solution)/shard_map/ckn,nj->ckj/dot_general | solution.py:49
  373.6 3.7 fusion.86
  377.2 3.7 fusion.84
  380.9 3.7 convolution_subtract_fusion
  384.6 3.9 convolution_add_fusion
  396.3 19.1 %all_to_all.44 = bf16[32,16,1024]{2,0,1:T(8,128)(2,1)S(1)} all-to-all(bf16[32,16,1024]{2,0,1:T(8,128)(2,1)S(1)} %copy.36), channel_id=1, replica_groups=mesh['ctx'=16,'tp'=8] {'ctx'}, dimensions={1} | all-to-all | bytes 2097152 | tf_op jit(solution)/shard_map/all_to_all | solution.py:109
  418.8 9.0 %convert_bitcast_fusion = bf16[4096,1024]{0,1:T(8,128)(2,1)} fusion(bf16[512,1024]{1,0:T(8,128)(2,1)S(1)} %fusion.41, bf16[512,4096]{1,0:T(8,128)(2,1)} %all-gather.5.cloned.1.call-done), kind=kOutput, calls=%fused_computation.2 | convolution fusion | flops 4299161600 | bytes 13631488 | tf_op jit(solution)/shard_map/cd,ct->dt/dot_general | solution.py:116
  427.8 114.3 %reduce-scatter.2.cloned.1.call-done = bf16[512,1024]{0,1:T(8,128)(2,1)} async-done(((bf16[4096,1024]{0,1:T(8,128)(2,1)}), bf16[512,1024]{0,1:T(8,128)(2,1)}) %reduce-scatter.2.cloned.1.call-update) | async-done | bytes 1048592 | tf_op jit(solution)/shard_map/reduce_scatter | solution.py:115
  (67 shorter events, 45.2 us)
Async XLA Ops:
  6.5 11.3 %copy-start.12 = (bf16[3,256,512]{2,1,0:T(8,128)(2,1)S(1)}, bf16[3,256,512]{2,1,0:T(8,128)(2,1)}, u32[]{:S(2)}) copy-start(bf16[3,256,512]{2,1,0:T(8,128)(2,1)} %param.7) | copy-start | bytes 2359300
  6.5 268.5 %all-gather.3.cloned.1.call-start = ((), (), s32[]{:S(2)}) async-start(), calls=%async_computation.5 | async-start | bytes 9437184 | tf_op jit(solution)/shard_map/all_gather | solution.py:80
  10.0 28.0 %all-to-all-start.2 = ((bf16[16,32,1024]{2,1,0:T(8,128)(2,1)}), bf16[16,32,1024]{2,1,0:T(8,128)(2,1)S(1)}, u32[]{:S(2)}, u32[]{:S(2)}) async-start(bf16[16,32,1024]{2,1,0:T(8,128)(2,1)} %bitcast.12), calls=%async_computation.2 | async-start | bytes 2097152 | tf_op jit(solution)/shard_map/all_to_all | solution.py:77
  44.0 7.3 %copy-start.13 = (f32[3,512,3]{1,2,0:T(4,128)S(1)}, f32[3,512,3]{1,2,0:T(4,128)}, u32[]{:S(2)}) copy-start(f32[3,512,3]{1,2,0:T(4,128)} %param.8) | copy-start | bytes 55300
  44.0 220.2 %all-to-all-start = ((bf16[16,3,256,512]{2,3,1,0:T(8,128)(2,1)}), bf16[16,3,256,512]{2,3,1,0:T(8,128)(2,1)}, u32[]{:S(2)}, u32[]{:S(2)}) async-start(bf16[16,3,256,512]{2,3,1,0:T(8,128)(2,1)} %stack.2), calls=%async_computation | async-start | bytes 25165824 | tf_op jit(solution)/shard_map/all_to_all | solution.py:83
  50.6 368.2 %all-gather.5.cloned.1.call-start = ((), (), s32[]{:S(2)}) async-start(), calls=%async_computation.6 | async-start | bytes 4456448 | tf_op jit(solution)/shard_map/all_gather | solution.py:114
  51.9 297.7 %copy-start.6 = (f32[256,128]{1,0:T(8,128)}, f32[256,128]{1,0:T(8,128)S(1)}, u32[]{:S(2)}) copy-start(f32[256,128]{1,0:T(8,128)S(1)} %get-tuple-element.12) | copy-start | bytes 393220
  51.9 297.7 %copy-start.9 = (f32[256,128]{1,0:T(8,128)}, f32[256,128]{1,0:T(8,128)S(1)}, u32[]{:S(2)}) copy-start(f32[256,128]{1,0:T(8,128)S(1)} %get-tuple-element.13) | copy-start | bytes 393220
  55.3 2.4 copy-start
  57.7 2.0 copy-start.2
  291.7 2.6 copy-start.4
  294.9 10.6 %collective-permute-start = (f32[3,512,2]{1,2,0:T(2,128)S(1)}, f32[3,512,2]{1,2,0:T(2,128)S(1)}, u32[]{:S(2)}, u32[]{:S(2)}) collective-permute-start(f32[3,512,2]{1,2,0:T(2,128)S(1)} %copy.27), channel_id=1, source_target_pairs={{0,8},{8,16},{16,24},{24,32},{32,40},{40,48},{48,56},{56,64},{64,7... | collective-permute-start | bytes 36872 | tf_op jit(solution)/shard_map/ppermute | solution.py:13
  315.0 2.6 copy-start.5
  319.0 24.5 %all-to-all-start.1 = ((bf16[16,32,1024]{2,1,0:T(8,128)(2,1)}), bf16[16,32,1024]{2,1,0:T(8,128)(2,1)S(1)}, u32[]{:S(2)}, u32[]{:S(2)}) async-start(bf16[16,32,1024]{2,1,0:T(8,128)(2,1)} %bitcast.4), calls=%async_computation.1 | async-start | bytes 2097152 | tf_op jit(solution)/shard_map/all_to_all | solution.py:101
  327.6 214.4 %reduce-scatter.2.cloned.1.call-start = ((), (), s32[]{:S(2)}) async-start(), calls=%async_computation.7 | async-start | bytes 9437184 | tf_op jit(solution)/shard_map/reduce_scatter | solution.py:115
  327.7 6.8 %copy-start.1 = (f32[256,32,128]{2,0,1:T(8,128)S(1)}, f32[256,32,128]{2,0,1:T(8,128)}, u32[]{:S(2)}) copy-start(f32[256,32,128]{2,0,1:T(8,128)} %copy-done) | copy-start | bytes 12582916
  327.7 6.8 %copy-start.3 = (f32[256,32,128]{2,0,1:T(8,128)S(1)}, f32[256,32,128]{2,0,1:T(8,128)}, u32[]{:S(2)}) copy-start(f32[256,32,128]{2,0,1:T(8,128)} %copy-done.2) | copy-start | bytes 12582916
  353.9 5.5 %copy-start.7 = (f32[256,128]{1,0:T(8,128)S(1)}, f32[256,128]{1,0:T(8,128)}, u32[]{:S(2)}) copy-start(f32[256,128]{1,0:T(8,128)} %copy-done.6) | copy-start | bytes 393220
  353.9 5.5 %copy-start.10 = (f32[256,128]{1,0:T(8,128)S(1)}, f32[256,128]{1,0:T(8,128)}, u32[]{:S(2)}) copy-start(f32[256,128]{1,0:T(8,128)} %copy-done.9) | copy-start | bytes 393220
  384.6 3.9 copy-start.8
  384.6 3.9 copy-start.11
  395.2 20.2 %copy-start.14 = (f32[512]{0:T(512)S(1)}, f32[512]{0:T(512)}, u32[]{:S(2)}) copy-start(f32[512]{0:T(512)} %param.10) | copy-start | bytes 6148
Sparse Core Ops, SparseCore 0:
  9.7 162.4 all-gather.2
  173.8 88.1 all-gather.4
  427.9 114.0 reduce-scatter.1
